TPU v7x, 32 devices: a whole 2x2x4 slice. The times are simulated.
32 devices in a mesh: pair: 8 (over z, y), aux: 4 (over x, core).
Axes of the slice: x: 2, y: 2, z: 4, core: 2. Of those that a mesh axis runs over, the one named last changes fastest.
Arguments:
- three_center: bfloat16 [1024, 32, 2048], P(('pair', 'aux')), may hold values from -1 to 1
- panel: bfloat16 [512, 64], P('pair'), may hold values from -6 to 6
- metric: float32 [32, 64, 64], P(('pair', 'aux')), may hold values from -0.5 to 1.6
- screen: int32 [8, 128, 1], P(None, 'aux'), may hold values from 0 to 7; in each aligned block of 32 rows (0 to 31, 32 to 63, ..., all dimensions but the last counted through in order) at most 8 rows name the same one
- pair_blocks: int32 [8, 128, 2], P(None, 'aux'), may hold values from 0 to 15
Outputs:
- fitted: bfloat16 [32, 512, 4096], P(('pair', 'aux'))
- exchange: float32 [512, 512], P(('pair', 'aux'))
Inputs may be any that keep to these rules, and one draw needn't show every extreme that they name: `screen`: in the list of one device no pair index is named by more than 8 slots, and in some lists one is named exactly 8 times.
All inputs are finite; a program needn't handle non-finite values.
Results may differ from a plain program's by a relative error of at most 0.0049.
Values may be sent and summed in bfloat16 or wider, within the bound.
A program may use at most 192 MiB of HBM per device.

v0:
```python
import jax
import jax.numpy as jnp
from jax import lax
from jax.sharding import PartitionSpec as P


def shards(three_center, panel, metric, screen, pair_blocks):
    pair_count = lax.axis_size("pair")
    column_count = lax.axis_size("aux")
    own_index = lax.axis_index("pair")
    slot_count = three_center.shape[0]
    basis_width = three_center.shape[1]
    aux_width = metric.shape[1]
    orbital_count = panel.shape[1]
    capacity = max(2, 2 * slot_count // pair_count)
    buffer_rows = pair_count * capacity
    whole_panel = lax.all_gather(panel, "pair", axis=0, tiled=True)
    basis_total = whole_panel.shape[0]
    block_count = basis_total // basis_width
    panel_blocks = whole_panel.reshape(block_count, basis_width * orbital_count)
    targets = screen[:, :, 0]
    mu_blocks = pair_blocks[:, :, 0]
    nu_blocks = pair_blocks[:, :, 1]
    slot_ids = jnp.arange(slot_count)
    earlier = slot_ids[None, :] < slot_ids[:, None]
    same_target = targets[:, :, None] == targets[:, None, :]
    ranks = jnp.sum(same_target & earlier[None, :, :], axis=2)
    own_targets = lax.dynamic_index_in_dim(targets, own_index, 0, keepdims=False)
    own_ranks = lax.dynamic_index_in_dim(ranks, own_index, 0, keepdims=False)
    own_nu = lax.dynamic_index_in_dim(nu_blocks, own_index, 0, keepdims=False)
    position = own_targets * capacity + own_ranks
    packing = (jnp.arange(buffer_rows)[:, None] == position[None, :]).astype(jnp.bfloat16)
    hits = (targets == own_index)[:, None, :] & (
        ranks[:, None, :] == jnp.arange(capacity)[None, :, None]
    )
    valid = jnp.any(hits, axis=2).reshape(buffer_rows)
    recv_mu = jnp.sum(jnp.where(hits, mu_blocks[:, None, :], 0), axis=2).reshape(buffer_rows)
    block_size = basis_width * aux_width * orbital_count
    own_pick = (own_nu[:, None] == jnp.arange(block_count)[None, :]).astype(jnp.bfloat16)
    own_panel = jnp.dot(own_pick, panel_blocks, preferred_element_type=jnp.float32).astype(
        jnp.bfloat16
    )
    own_panel = own_panel.reshape(slot_count, basis_width, orbital_count)
    blocks_local = three_center.reshape(slot_count, basis_width, aux_width, basis_width)
    transformed = jnp.einsum(
        "smqn,sni->smqi", blocks_local, own_panel, preferred_element_type=jnp.float32
    )
    transformed = transformed.astype(jnp.bfloat16).reshape(slot_count, block_size)
    outgoing = jnp.dot(packing, transformed, preferred_element_type=jnp.float32).astype(
        jnp.bfloat16
    )
    outgoing = outgoing.reshape(pair_count, capacity, block_size)
    arrived = lax.all_to_all(outgoing, "pair", split_axis=0, concat_axis=0, tiled=True)
    received = arrived.reshape(buffer_rows, block_size)
    placing = ((recv_mu[None, :] == jnp.arange(block_count)[:, None]) & valid[None, :]).astype(
        jnp.bfloat16
    )
    coefficients = jnp.dot(placing, received, preferred_element_type=jnp.float32)
    coefficients = coefficients.reshape(basis_total, aux_width, orbital_count)
    fitted = jnp.einsum("pq,rqi->rpi", metric[0], coefficients, precision=lax.Precision.HIGHEST)
    fitted = fitted.astype(jnp.bfloat16).reshape(basis_total, aux_width * orbital_count)
    summed_rows = lax.psum_scatter(
        lax.dot_general(
            fitted, fitted, (((1,), (1,)), ((), ())), preferred_element_type=jnp.float32
        ),
        ("pair", "aux"),
        scatter_dimension=0,
        tiled=True,
    )
    norm_factor = 1.0 / (pair_count * column_count * aux_width * orbital_count)
    return (fitted[None], summed_rows * norm_factor)


def solution(mesh):
    return jax.shard_map(
        shards,
        mesh=mesh,
        in_specs=(
            P(("pair", "aux"), None, None),
            P("pair", None),
            P(("pair", "aux"), None, None),
            P(None, "aux", None),
            P(None, "aux", None),
        ),
        out_specs=(P(("pair", "aux"), None, None), P(("pair", "aux"), None)),
        check_vma=False,
    )
```

profile of v0, /device:TPU:0, one launch (start us, length us, event | category | flops | bytes accessed | tf_op | source)
XLA Modules:
  0.0 698.0 jit_solution(11234505883591912201)
XLA Ops:
  7.2 0.0 copy-start
  7.2 0.8 fusion.18
  8.0 1.1 convert_reduce_fusion
  9.0 0.7 fusion.17
  9.7 32.5 %all_gather.3 = bf16[512,64]{1,0:T(8,128)(2,1)S(1)} all-gather(bf16[64,64]{1,0:T(8,128)(2,1)} %param.6), channel_id=1, replica_groups=mesh['pair'=8,'aux'=4] {'pair'}, dimensions={0}, use_global_device_ids=true | all-gather | bytes 73728 | tf_op jit(solution)/shard_map/all_gather | solution.py:17
  42.2 0.2 reshape.66
  42.4 0.2 convolution_convert_fusion.1
  42.6 0.2 reshape.73
  42.9 19.5 %reshape.68 = bf16[32,32,64,32]{3,2,1,0:T(8,128)(2,1)} reshape(bf16[32,32,2048]{2,1,0:T(8,128)(2,1)} %param.5) | data formatting | bytes 8388608 | tf_op jit(solution)/shard_map/reshape | solution.py:44
  62.4 21.9 %convert_bitcast_fusion = bf16[32,32,64,64]{2,3,1,0:T(8,128)(2,1)} fusion(bf16[32,32,64,32]{3,2,1,0:T(8,128)(2,1)} %reshape.68, bf16[32,32,64,1]{2,1,0,3:T(8,128)(2,1)S(1)} %reshape.73), kind=kOutput, calls=%fused_computation.4 | convolution fusion | flops 272629760 | bytes 12713984 | tf_op jit(solution)/shard_map/smqn,sni->smqi/dot_general | solution.py:45
  84.3 22.5 %copy.19 = bf16[32,32,64,64]{3,2,1,0:T(8,128)(2,1)} copy(bf16[32,32,64,64]{2,3,1,0:T(8,128)(2,1)} %convert_bitcast_fusion) | data formatting | bytes 16777216 | tf_op jit(solution)/shard_map/convert_element_type | solution.py:48
  106.8 16.0 %reshape.69 = bf16[32,131072]{1,0:T(8,128)(2,1)} reshape(bf16[32,32,64,64]{3,2,1,0:T(8,128)(2,1)} %copy.19) | data formatting | bytes 16777216 | tf_op jit(solution)/shard_map/reshape | solution.py:48
  122.8 11.4 %fusion = bf16[8,8,131072]{2,1,0:T(8,128)(2,1)} fusion(bf16[32,131072]{1,0:T(8,128)(2,1)} %reshape.69, s32[32]{0:T(128)S(1)} %fusion.17), kind=kOutput, calls=%fused_computation.1 | convolution fusion | flops 545261568 | bytes 25165952 | tf_op jit(solution)/shard_map/dot_general | solution.py:49
  134.2 0.0 copy-start.2
  134.2 5.9 all-to-all-start
  140.1 0.2 reduce-scatter.2.cloned.1.call-start
  140.3 0.0 copy-done.2
  140.4 0.2 fusion.6
  140.6 0.1 and.31
  140.7 0.2 select_reduce_fusion
  140.9 0.1 eq.89
  141.0 356.2 %all-to-all-done = bf16[8,8,131072]{2,1,0:T(8,128)(2,1)} async-done(((bf16[8,8,131072]{2,1,0:T(8,128)(2,1)}), bf16[8,8,131072]{2,1,0:T(8,128)(2,1)}, u32[]{:S(2)}, u32[]{:S(2)}) %all-to-all-start) | async-done | bytes 16777248 | tf_op jit(solution)/shard_map/all_to_all | solution.py:53
  497.2 11.3 %fusion.1 = f32[16,131072]{1,0:T(8,128)} fusion(bf16[8,8,131072]{2,1,0:T(8,128)(2,1)} %all-to-all-done, s32[64]{0:T(128)S(1)} %eq.89, pred[64]{0:T(512)(128)(4,1)S(1)} %and.31), kind=kOutput, calls=%fused_computation.2 | convolution fusion | flops 268437504 | bytes 25166144 | tf_op jit(solution)/shard_map/dot_general | solution.py:58
  508.4 17.4 %reshape.72 = f32[512,64,64]{2,1,0:T(8,128)} reshape(f32[16,131072]{1,0:T(8,128)} %fusion.1) | data formatting | bytes 16777216 | tf_op jit(solution)/shard_map/reshape | solution.py:59
  525.8 13.8 %copy.20 = f32[512,64,64]{0,1,2:T(8,128)} copy(f32[512,64,64]{2,1,0:T(8,128)} %reshape.72) | data formatting | bytes 16777216 | tf_op jit(solution)/shard_map/reshape | solution.py:59
  539.6 0.0 copy-done
  539.6 10.4 %convert_bitcast_fusion.1 = bf16[512,64,64]{0,1,2:T(8,128)(2,1)S(1)} fusion(f32[512,64,64]{0,1,2:T(8,128)} %copy.20, f32[1,64,64]{2,1,0:T(8,128)S(1)} %copy-done), kind=kOutput, calls=%fused_computation.5 | convolution fusion | flops 1612709888 | bytes 12599296 | tf_op jit(solution)/shard_map/pq,rqi->rpi/dot_general | solution.py:60
  550.1 0.0 copy-start.1
  550.1 2.0 copy-done.1
  552.1 3.3 convolution_bitcast_fusion
  555.4 0.0 reduce-scatter.2.cloned.1.call-update
  555.4 6.5 copy.21
  561.9 6.3 copy.22
  568.2 121.6 %reduce-scatter.2.cloned.1.call-done = f32[16,512]{1,0:T(8,128)} async-done(((f32[512,512]{1,0:T(8,128)}), f32[16,512]{1,0:T(8,128)}) %reduce-scatter.2.cloned.1.call-update) | async-done | bytes 32784 | tf_op jit(solution)/shard_map/reduce_scatter | solution.py:62
  689.8 1.4 broadcast_multiply_fusion
  (3 shorter events, 0.0 us)
Async XLA Ops:
  7.2 532.5 %copy-start = (f32[1,64,64]{2,1,0:T(8,128)S(1)}, f32[1,64,64]{2,1,0:T(8,128)}, u32[]{:S(2)}) copy-start(f32[1,64,64]{2,1,0:T(8,128)} %param.7) | copy-start | bytes 49156
  134.2 6.1 copy-start.2
  134.2 362.9 %all-to-all-start = ((bf16[8,8,131072]{2,1,0:T(8,128)(2,1)}), bf16[8,8,131072]{2,1,0:T(8,128)(2,1)}, u32[]{:S(2)}, u32[]{:S(2)}) async-start(bf16[8,8,131072]{2,1,0:T(8,128)(2,1)} %fusion), calls=%async_computation | async-start | bytes 33554432 | tf_op jit(solution)/shard_map/all_to_all | solution.py:53
  140.1 549.7 %reduce-scatter.2.cloned.1.call-start = ((), (), s32[]{:S(2)}) async-start(), calls=%async_computation.2 | async-start | bytes 1081344 | tf_op jit(solution)/shard_map/reduce_scatter | solution.py:62
  550.1 2.0 copy-start.1
Sparse Core Ops, SparseCore 0:
  555.5 134.2 reduce-scatter.1
where the time goes:
time: 700 us; the launch traced here: 698 us
  waiting for transfers between devices  478 us (68%)
  local copies, waits for them, and re-layouts  105 us (15%)
  matrix products  58.6 us (8%)
  blocking collectives  32.5 us (5%)
  between operations  14.1 us (2%)
    all_to_all x1, waiting for transfers between devices, shards(): lax.all_to_all(outgoing, 'pair', split_axis=0, concat_axis=0, tiled=True)  356 us
    reduce_scatter x1, waiting for transfers between devices, shards(): lax.psum_scatter(lax.dot_general(fitted, fitted, (((1,), (1,)), ((), ()))...  122 us
    all_gather x1, blocking collectives, shards(): whole_panel = lax.all_gather(panel, 'pair', axis=0, tiled=True)  32.5 us
    reshape x2, local copies, waits for them, and re-layouts, shards(): coefficients = coefficients.reshape(basis_total, aux_width, orbital_count)  31.2 us
    convert_element_type x1, local copies, waits for them, and re-layouts, shards(): transformed.astype(jnp.bfloat16).reshape(slot_count, block_size)  22.5 us
    dot_general x1, matrix products, shards(): jnp.einsum('smqn,sni->smqi', blocks_local, own_panel, preferred_element_t...  21.9 us
    reshape x1, local copies, waits for them, and re-layouts, shards(): three_center.reshape(slot_count, basis_width, aux_width, basis_width)  19.5 us
    reshape x1, local copies, waits for them, and re-layouts, shards(): transformed.astype(jnp.bfloat16).reshape(slot_count, block_size)  16 us
  transfers between devices with their start and end apart: 2, of which 2 were waited for; matrix products, arithmetic and copies ran while one was open for 2% of the time, Pallas kernels for 0%

commit v1 on v0

v1 whole, which is shorter than its diff:
```python
import functools

import jax
import jax.numpy as jnp
from jax import lax
from jax.experimental import pallas as pl
from jax.experimental.pallas import tpu as pltpu
from jax.sharding import PartitionSpec as P

MESH = pl.DeviceIdType.MESH
QG = 8
IG = 16


def pack_kernel(pair_count, capacity, base, table_ref, tc_ref, packed_ref, counts, sems):
    me = lax.axis_index("pair")
    slot_count = tc_ref.shape[0]

    def clear(i, _):
        counts[i] = 0
        return 0

    lax.fori_loop(0, pair_count, clear, 0)

    def start(s, _):
        target = lax.div(table_ref[me, s], base * base)
        rank = counts[target]
        counts[target] = rank + 1
        pltpu.make_async_copy(
            tc_ref.at[s], packed_ref.at[target * capacity + rank], sems.at[s]
        ).start()
        return 0

    lax.fori_loop(0, slot_count, start, 0)

    def finish(s, _):
        pltpu.make_async_copy(tc_ref.at[s], packed_ref.at[0], sems.at[s]).wait()
        return 0

    lax.fori_loop(0, slot_count, finish, 0)


def exchange_kernel(n, packed_ref, recv_ref, send_sems, recv_sems, own_sem):
    me = lax.axis_index("pair")
    barrier = pltpu.get_barrier_semaphore()
    for k in range(1, n):
        pl.semaphore_signal(
            barrier, inc=1, device_id={"pair": lax.rem(me + k, n)}, device_id_type=MESH
        )
    pl.semaphore_wait(barrier, n - 1)
    copies = []
    for k in range(1, n):
        dst = lax.rem(me + k, n)
        copy = pltpu.make_async_remote_copy(
            src_ref=packed_ref.at[dst],
            dst_ref=recv_ref.at[me],
            send_sem=send_sems.at[k],
            recv_sem=recv_sems.at[k],
            device_id={"pair": dst},
            device_id_type=MESH,
        )
        copy.start()
        copies.append(copy)
    own = pltpu.make_async_copy(packed_ref.at[me], recv_ref.at[me], own_sem)
    own.start()
    own.wait()
    for copy in copies:
        copy.wait()


def iota(shape, axis):
    return lax.broadcasted_iota(jnp.int32, shape, axis)


def fit_kernel(
    capacity,
    table_ref,
    panel_ref,
    metric_ref,
    recv_ref,
    fitted_ref,
    gram_ref,
    recv_buf,
    weights,
    metric_hi,
    metric_lo,
    coeff,
    entries,
    recv_sem,
):
    me = lax.axis_index("pair")
    pair_count, slot_count = table_ref.shape
    width = recv_buf.shape[1]
    aux = metric_ref.shape[1]
    orbitals = panel_ref.shape[1]
    basis = panel_ref.shape[0]
    block_count = basis // width
    chunks = aux // QG
    groups = orbitals // IG
    depth = QG * width
    wide = QG * orbitals
    lanes = QG * IG

    load = pltpu.make_async_copy(recv_ref, recv_buf, recv_sem)
    load.start()

    def per_source(p, found):
        def per_slot(s, carry):
            found, rank = carry
            code = table_ref[p, s]
            mine = lax.div(code, block_count * block_count) == me

            @pl.when(mine)
            def _():
                entries[0, found] = p * capacity + rank
                entries[1, found] = lax.rem(lax.div(code, block_count), block_count)
                entries[2, found] = lax.rem(code, block_count)

            step = mine.astype(jnp.int32)
            return found + step, rank + step

        found, _ = lax.fori_loop(0, slot_count, per_slot, (found, 0))
        return found

    found = lax.fori_loop(0, pair_count, per_source, 0)
    entries[0, found] = 0
    entries[1, found] = block_count
    entries[2, found] = 0

    expand = (
        iota((orbitals, wide), 0) == iota((orbitals, wide), 1) // QG
    ).astype(jnp.bfloat16)
    diagonal = iota((depth, wide), 0) // width == iota((depth, wide), 1) % QG
    for n in range(block_count):
        block = panel_ref[n * width : (n + 1) * width, :]
        spread = jnp.dot(block, expand, preferred_element_type=jnp.float32)
        spread = jnp.concatenate([spread] * QG, axis=0)
        weights[n] = jnp.where(diagonal, spread, 0.0).astype(jnp.bfloat16)

    size = aux * IG
    metric = metric_ref[0]
    high = metric.astype(jnp.bfloat16)
    low = (metric - high.astype(jnp.float32)).astype(jnp.bfloat16)
    row_aux = (iota((size, aux), 0) // lanes) * QG + iota((size, aux), 0) % QG
    pick_row = (row_aux == iota((size, aux), 1)).astype(jnp.bfloat16)
    pick_col = (iota((aux, size), 0) == iota((aux, size), 1) // IG).astype(jnp.bfloat16)
    same = (iota((size, size), 0) % lanes) // QG == iota((size, size), 1) % IG
    for part, out in ((high, metric_hi), (low, metric_lo)):
        rows = lax.dot_general(
            pick_row, part, (((1,), (1,)), ((), ())), preferred_element_type=jnp.float32
        ).astype(jnp.bfloat16)
        full = jnp.dot(rows, pick_col, preferred_element_type=jnp.float32)
        out[...] = jnp.where(same, full, 0.0).astype(jnp.bfloat16)

    coeff[...] = jnp.zeros_like(coeff)
    load.wait()

    def add(k):
        entry, mu, nu = entries[0, k], entries[1, k], entries[2, k]
        block = recv_buf[entry]
        stacked = jnp.concatenate(
            [block[:, c * depth : (c + 1) * depth] for c in range(chunks)], axis=0
        )
        half = jnp.dot(stacked, weights[nu], preferred_element_type=jnp.float32)
        rows = pl.ds(pl.multiple_of(mu * width, width), width)
        for c in range(chunks):
            coeff[c, rows, :] += half[c * width : (c + 1) * width, :]

    def add_two(j, _):
        add(2 * j)
        add(2 * j + 1)
        return 0

    lax.fori_loop(0, (found + 1) // 2, add_two, 0)

    source = iota((wide, wide), 0)
    dest = iota((wide, wide), 1)
    wanted = (
        (dest % orbitals) // IG * lanes + dest // orbitals * IG + dest % IG
    )
    order = (source == wanted).astype(jnp.bfloat16)
    step = min(256, basis)
    for r in range(0, basis, step):
        parts = []
        for g in range(groups):
            piece = jnp.concatenate(
                [coeff[c, r : r + step, g * lanes : (g + 1) * lanes] for c in range(chunks)],
                axis=1,
            ).astype(jnp.bfloat16)
            out = jnp.dot(piece, metric_hi[...], preferred_element_type=jnp.float32)
            out += jnp.dot(piece, metric_lo[...], preferred_element_type=jnp.float32)
            parts.append(out.astype(jnp.bfloat16))
        for o in range(chunks):
            mixed = jnp.concatenate(
                [part[:, o * lanes : (o + 1) * lanes] for part in parts], axis=1
            )
            fitted_ref[0, r : r + step, o * wide : (o + 1) * wide] = jnp.dot(
                mixed, order, preferred_element_type=jnp.float32
            ).astype(jnp.bfloat16)
    gram_ref[...] = lax.dot_general(
        fitted_ref[0],
        fitted_ref[0],
        (((1,), (1,)), ((), ())),
        preferred_element_type=jnp.float32,
    )


def shards(three_center, panel, metric, screen, pair_blocks):
    pair_count = lax.axis_size("pair")
    column_count = lax.axis_size("aux")
    slot_count, width, flat = three_center.shape
    aux = metric.shape[1]
    orbitals = panel.shape[1]
    capacity = max(2, 2 * slot_count // pair_count)
    rows = pair_count * capacity
    whole_panel = lax.all_gather(panel, "pair", axis=0, tiled=True)
    basis = whole_panel.shape[0]
    block_count = basis // width
    table = (screen[:, :, 0] * block_count + pair_blocks[:, :, 0]) * block_count
    table += pair_blocks[:, :, 1]
    smem = pl.BlockSpec(memory_space=pltpu.SMEM)
    vmem = pl.BlockSpec(memory_space=pltpu.VMEM)
    hbm = pl.BlockSpec(memory_space=pl.ANY)

    packed = pl.pallas_call(
        functools.partial(pack_kernel, pair_count, capacity, block_count),
        out_shape=jax.ShapeDtypeStruct((rows, width, flat), jnp.bfloat16),
        in_specs=[smem, hbm],
        out_specs=hbm,
        scratch_shapes=[
            pltpu.SMEM((pair_count,), jnp.int32),
            pltpu.SemaphoreType.DMA((slot_count,)),
        ],
        name="pack",
    )(table, three_center)

    received = pl.pallas_call(
        functools.partial(exchange_kernel, pair_count),
        out_shape=jax.ShapeDtypeStruct((pair_count, capacity, width, flat), jnp.bfloat16),
        in_specs=[hbm],
        out_specs=hbm,
        scratch_shapes=[
            pltpu.SemaphoreType.DMA((pair_count,)),
            pltpu.SemaphoreType.DMA((pair_count,)),
            pltpu.SemaphoreType.DMA,
        ],
        compiler_params=pltpu.CompilerParams(collective_id=0, has_side_effects=True),
        name="exchange_blocks",
    )(packed.reshape(pair_count, capacity, width, flat))

    size = aux * IG
    fitted, gram = pl.pallas_call(
        functools.partial(fit_kernel, capacity),
        out_shape=(
            jax.ShapeDtypeStruct((1, basis, aux * orbitals), jnp.bfloat16),
            jax.ShapeDtypeStruct((basis, basis), jnp.float32),
        ),
        in_specs=[smem, vmem, vmem, hbm],
        out_specs=(vmem, vmem),
        scratch_shapes=[
            pltpu.VMEM((rows, width, flat), jnp.bfloat16),
            pltpu.VMEM((block_count, QG * width, QG * orbitals), jnp.bfloat16),
            pltpu.VMEM((size, size), jnp.bfloat16),
            pltpu.VMEM((size, size), jnp.bfloat16),
            pltpu.VMEM((aux // QG, basis + width, QG * orbitals), jnp.float32),
            pltpu.SMEM((3, rows + 8), jnp.int32),
            pltpu.SemaphoreType.DMA,
        ],
        compiler_params=pltpu.CompilerParams(vmem_limit_bytes=44 * 2**20),
        name="fit",
    )(table, whole_panel, metric, received.reshape(rows, width, flat))

    summed_rows = lax.psum_scatter(gram, ("pair", "aux"), scatter_dimension=0, tiled=True)
    norm_factor = 1.0 / (pair_count * column_count * aux * orbitals)
    return fitted, summed_rows * norm_factor


def solution(mesh):
    return jax.shard_map(
        shards,
        mesh=mesh,
        in_specs=(
            P(("pair", "aux"), None, None),
            P("pair", None),
            P(("pair", "aux"), None, None),
            P(None, "aux", None),
            P(None, "aux", None),
        ),
        out_specs=(P(("pair", "aux"), None, None), P(("pair", "aux"), None)),
        check_vma=False,
    )
```

time: 700 us -> 532 us (0.76)
  waiting for transfers between devices: 478 us -> 143 us
  Pallas kernels: 0 us -> 295 us
  local copies, waits for them, and re-layouts: 105 us -> 4.18 us
  matrix products: 58.6 us -> 0 us
  blocking collectives: 32.5 us -> 75 us
    all_to_all x1 -> x0, waiting for transfers between devices: 356 us -> none  [shards(): lax.all_to_all(outgoing, 'pair', split_axis=0, concat_axis=0, tiled=True)]
    pallas_call x0 -> x3, Pallas kernels: none -> 295 us  [the longest x1 141 us: shards(): pl.pallas_call(functools.partial(exchange_kernel, pair_count), out_shape=...]
    reshape x6 -> x0, local copies, waits for them, and re-layouts: 67.1 us -> none  [the longest x2 31.2 us: shards(): coefficients = coefficients.reshape(basis_total, aux_width, orbital_count)]
    dot_general x6 -> x0, matrix products: 58.6 us -> none  [the longest x1 21.9 us: shards(): jnp.einsum('smqn,sni->smqi', blocks_local, own_panel, preferred_element_t...]
    all_gather x1, blocking collectives: 32.5 us -> 75 us  [shards(): whole_panel = lax.all_gather(panel, 'pair', axis=0, tiled=True)]
    convert_element_type x2 -> x0, local copies, waits for them, and re-layouts: 29 us -> none  [the longest x1 22.5 us: shards(): transformed.astype(jnp.bfloat16).reshape(slot_count, block_size)]
    reduce_scatter x1, waiting for transfers between devices: 122 us -> 143 us  [shards(): lax.psum_scatter(gram, ('pair', 'aux'), scatter_dimension=0, tiled=True)]
  transfers between devices with their start and end apart: 2 -> 1, of which waited for: 2 -> 1; matrix products, arithmetic and copies ran while one was open for 2% -> 0% of each run, Pallas kernels for 0% -> 0%
where the time goes in v1:
time: 532 us; the launch traced here: 535 us
  Pallas kernels  295 us (55%)
  waiting for transfers between devices  143 us (27%)
  blocking collectives  75 us (14%)
  between operations  14.1 us (3%)
    reduce_scatter x1, waiting for transfers between devices, shards(): lax.psum_scatter(gram, ('pair', 'aux'), scatter_dimension=0, tiled=True)  143 us
    pallas_call x1, Pallas kernels, shards(): pl.pallas_call(functools.partial(exchange_kernel, pair_count), out_shape=...  141 us
    pallas_call x1, Pallas kernels, shards(): pl.pallas_call(functools.partial(pack_kernel, pair_count, capacity, block...  129 us
    all_gather x1, blocking collectives, shards(): whole_panel = lax.all_gather(panel, 'pair', axis=0, tiled=True)  75 us
    pallas_call x1, Pallas kernels, shards(): pl.pallas_call(functools.partial(fit_kernel, capacity), out_shape=(jax.Sh...  24.8 us
  transfers between devices with their start and end apart: 1, of which 1 were waited for; matrix products, arithmetic and copies ran while one was open for 0% of the time, Pallas kernels for 0%

profile of v1, /device:TPU:0, one launch (start us, length us, event | category | flops | bytes accessed | tf_op | source)
XLA Modules:
  0.0 534.7 jit_solution(4768499399996230740)
XLA Ops:
  7.2 0.0 reduce-scatter.2.cloned.1.call-start
  7.2 0.8 fusion
  8.0 1.3 add_bitcast_fusion.table_ref
  9.3 129.2 %pack.1 = bf16[64,32,2048]{2,1,0:T(8,128)(2,1)} custom-call(s32[8,32]{1,0:T(8,128)} %add_bitcast_fusion.table_ref, bf16[32,32,2048]{2,1,0:T(8,128)(2,1)} %tc_ref.1), custom_call_target="tpu_custom_call" | custom-call | tf_op jit(solution)/shard_map/pack/pallas_call | solution.py:225
  138.5 0.0 copy-start.3
  138.5 0.0 copy-start.1
  138.5 0.0 copy-start.2
  138.6 141.3 %exchange_blocks.1 = bf16[8,8,32,2048]{3,2,1,0:T(8,128)(2,1)} custom-call(bf16[8,8,32,2048]{3,2,1,0:T(8,128)(2,1)} %bitcast.8), custom_call_target="tpu_custom_call" | custom-call | tf_op jit(solution)/shard_map/exchange_blocks/pallas_call | solution.py:237
  279.9 0.0 copy-done.3
  279.9 75.0 %all_gather.3.panel_ref = bf16[512,64]{1,0:T(8,128)(2,1)S(1)} all-gather(bf16[64,64]{1,0:T(8,128)(2,1)S(1)} %copy-done.3), channel_id=1, replica_groups=mesh['pair'=8,'aux'=4] {'pair'}, dimensions={0}, use_global_device_ids=true | all-gather | bytes 73728 | tf_op jit(solution)/shard_map/all_gather | solution.py:216
  354.9 0.0 copy-done.1
  354.9 0.0 copy-done.2
  354.9 0.0 copy-start
  354.9 3.4 copy-done
  358.3 24.8 %fit.1 = (bf16[1,512,4096]{2,1,0:T(8,128)(2,1)}, f32[512,512]{1,0:T(8,128)}) custom-call(s32[8,32]{1,0:T(8,128)S(1)} %copy-done.1, bf16[512,64]{1,0:T(8,128)(2,1)S(1)} %all_gather.3.panel_ref, f32[1,64,64]{2,1,0:T(8,128)S(1)} %copy-done.2, bf16[64,32,2048]{2,1,0:T(8,128)(2,1)S(1)} %bitcast.7), custom_call_target="tpu_custom_call" | custom-call | tf_op jit(solution)/shard_map/fit/pallas_call | solution.py:252
  383.1 0.0 reduce-scatter.2.cloned.1.call-update
  383.2 143.3 %reduce-scatter.2.cloned.1.call-done = f32[16,512]{1,0:T(8,128)} async-done(((f32[512,512]{1,0:T(8,128)}), f32[16,512]{1,0:T(8,128)}) %reduce-scatter.2.cloned.1.call-update) | async-done | bytes 32784 | tf_op jit(solution)/shard_map/reduce_scatter | solution.py:273
  526.5 1.4 broadcast_multiply_fusion
Async XLA Ops:
  7.2 519.3 %reduce-scatter.2.cloned.1.call-start = ((), (), s32[]{:S(2)}) async-start(), calls=%async_computation.1 | async-start | bytes 1081344 | tf_op jit(solution)/shard_map/reduce_scatter | solution.py:273
  138.5 141.4 %copy-start.3 = (bf16[64,64]{1,0:T(8,128)(2,1)S(1)}, bf16[64,64]{1,0:T(8,128)(2,1)}, u32[]{:S(2)}) copy-start(bf16[64,64]{1,0:T(8,128)(2,1)} %param.6) | copy-start | bytes 24580
  138.5 216.4 %copy-start.1 = (s32[8,32]{1,0:T(8,128)S(1)}, s32[8,32]{1,0:T(8,128)}, u32[]{:S(2)}) copy-start(s32[8,32]{1,0:T(8,128)} %add_bitcast_fusion.table_ref) | copy-start | bytes 3076
  138.5 216.4 %copy-start.2 = (f32[1,64,64]{2,1,0:T(8,128)S(1)}, f32[1,64,64]{2,1,0:T(8,128)}, u32[]{:S(2)}) copy-start(f32[1,64,64]{2,1,0:T(8,128)} %metric_ref.1) | copy-start | bytes 49156
  354.9 3.4 copy-start
Sparse Core Ops, SparseCore 0:
  383.3 143.1 reduce-scatter.1

commit v2 on v1

--- a/solution.py
+++ b/solution.py
@@ -40,8 +40,21 @@
     lax.fori_loop(0, slot_count, finish, 0)
 
 
-def exchange_kernel(n, packed_ref, recv_ref, send_sems, recv_sems, own_sem):
+def exchange_kernel(
+    n,
+    packed_ref,
+    panel_ref,
+    recv_ref,
+    whole_ref,
+    send_sems,
+    recv_sems,
+    panel_send,
+    panel_recv,
+    own_sem,
+):
     me = lax.axis_index("pair")
+    rows = panel_ref.shape[0]
+    mine = pl.ds(pl.multiple_of(me * rows, rows), rows)
     barrier = pltpu.get_barrier_semaphore()
     for k in range(1, n):
         pl.semaphore_signal(
@@ -49,6 +62,17 @@
         )
     pl.semaphore_wait(barrier, n - 1)
     copies = []
+    for k in range(1, n):
+        copy = pltpu.make_async_remote_copy(
+            src_ref=panel_ref,
+            dst_ref=whole_ref.at[mine],
+            send_sem=panel_send.at[k],
+            recv_sem=panel_recv.at[k],
+            device_id={"pair": lax.rem(me + k, n)},
+            device_id_type=MESH,
+        )
+        copy.start()
+        copies.append(copy)
     for k in range(1, n):
         dst = lax.rem(me + k, n)
         copy = pltpu.make_async_remote_copy(
@@ -63,6 +87,7 @@
         copies.append(copy)
     own = pltpu.make_async_copy(packed_ref.at[me], recv_ref.at[me], own_sem)
     own.start()
+    whole_ref[mine, :] = panel_ref[...]
     own.wait()
     for copy in copies:
         copy.wait()
@@ -205,6 +230,75 @@
     )
 
 
+def reduce_kernel(
+    n,
+    columns,
+    norm_factor,
+    gram_ref,
+    out_ref,
+    send_one,
+    recv_one,
+    partial,
+    send_two,
+    recv_two,
+    send_one_sems,
+    recv_one_sems,
+    send_two_sems,
+    recv_two_sems,
+):
+    me = lax.axis_index("pair")
+    col = lax.axis_index("aux")
+    barrier = pltpu.get_barrier_semaphore()
+    for k in range(1, columns):
+        pl.semaphore_signal(
+            barrier, inc=1, device_id={"aux": lax.rem(col + k, columns)}, device_id_type=MESH
+        )
+    for k in range(1, n):
+        pl.semaphore_signal(
+            barrier, inc=1, device_id={"pair": lax.rem(me + k, n)}, device_id_type=MESH
+        )
+    for a in range(columns):
+        send_one[a] = gram_ref[:, a].astype(send_one.dtype)
+    pl.semaphore_wait(barrier, columns + n - 2)
+    copies = []
+    for k in range(1, columns):
+        dst = lax.rem(col + k, columns)
+        copy = pltpu.make_async_remote_copy(
+            src_ref=send_one.at[dst],
+            dst_ref=recv_one.at[k - 1],
+            send_sem=send_one_sems.at[k],
+            recv_sem=recv_one_sems.at[k],
+            device_id={"aux": dst},
+            device_id_type=MESH,
+        )
+        copy.start()
+        copies.append(copy)
+    total = gram_ref[:, col]
+    for k, copy in enumerate(copies):
+        copy.wait()
+        total += recv_one[k].astype(jnp.float32)
+    partial[...] = total
+    send_two[...] = total.astype(send_two.dtype)
+    copies = []
+    for k in range(1, n):
+        dst = lax.rem(me + k, n)
+        copy = pltpu.make_async_remote_copy(
+            src_ref=send_two.at[dst],
+            dst_ref=recv_two.at[k - 1],
+            send_sem=send_two_sems.at[k],
+            recv_sem=recv_two_sems.at[k],
+            device_id={"pair": dst},
+            device_id_type=MESH,
+        )
+        copy.start()
+        copies.append(copy)
+    total = partial[me]
+    for k, copy in enumerate(copies):
+        copy.wait()
+        total += recv_two[k].astype(jnp.float32)
+    out_ref[...] = total * norm_factor
+
+
 def shards(three_center, panel, metric, screen, pair_blocks):
     pair_count = lax.axis_size("pair")
     column_count = lax.axis_size("aux")
@@ -213,8 +307,7 @@
     orbitals = panel.shape[1]
     capacity = max(2, 2 * slot_count // pair_count)
     rows = pair_count * capacity
-    whole_panel = lax.all_gather(panel, "pair", axis=0, tiled=True)
-    basis = whole_panel.shape[0]
+    basis = pair_count * panel.shape[0]
     block_count = basis // width
     table = (screen[:, :, 0] * block_count + pair_blocks[:, :, 0]) * block_count
     table += pair_blocks[:, :, 1]
@@ -226,27 +319,33 @@
         functools.partial(pack_kernel, pair_count, capacity, block_count),
         out_shape=jax.ShapeDtypeStruct((rows, width, flat), jnp.bfloat16),
         in_specs=[smem, hbm],
-        out_specs=hbm,
+        out_specs=vmem,
         scratch_shapes=[
             pltpu.SMEM((pair_count,), jnp.int32),
             pltpu.SemaphoreType.DMA((slot_count,)),
         ],
+        compiler_params=pltpu.CompilerParams(vmem_limit_bytes=16 * 2**20),
         name="pack",
     )(table, three_center)
 
-    received = pl.pallas_call(
+    received, whole_panel = pl.pallas_call(
         functools.partial(exchange_kernel, pair_count),
-        out_shape=jax.ShapeDtypeStruct((pair_count, capacity, width, flat), jnp.bfloat16),
-        in_specs=[hbm],
-        out_specs=hbm,
+        out_shape=(
+            jax.ShapeDtypeStruct((pair_count, capacity, width, flat), jnp.bfloat16),
+            jax.ShapeDtypeStruct((basis, orbitals), jnp.bfloat16),
+        ),
+        in_specs=[hbm, vmem],
+        out_specs=(hbm, vmem),
         scratch_shapes=[
+            pltpu.SemaphoreType.DMA((pair_count,)),
+            pltpu.SemaphoreType.DMA((pair_count,)),
             pltpu.SemaphoreType.DMA((pair_count,)),
             pltpu.SemaphoreType.DMA((pair_count,)),
             pltpu.SemaphoreType.DMA,
         ],
         compiler_params=pltpu.CompilerParams(collective_id=0, has_side_effects=True),
         name="exchange_blocks",
-    )(packed.reshape(pair_count, capacity, width, flat))
+    )(packed.reshape(pair_count, capacity, width, flat), panel)
 
     size = aux * IG
     fitted, gram = pl.pallas_call(
@@ -270,9 +369,30 @@
         name="fit",
     )(table, whole_panel, metric, received.reshape(rows, width, flat))
 
-    summed_rows = lax.psum_scatter(gram, ("pair", "aux"), scatter_dimension=0, tiled=True)
     norm_factor = 1.0 / (pair_count * column_count * aux * orbitals)
-    return fitted, summed_rows * norm_factor
+    part = basis // (pair_count * column_count)
+    exchange = pl.pallas_call(
+        functools.partial(reduce_kernel, pair_count, column_count, norm_factor),
+        out_shape=jax.ShapeDtypeStruct((part, basis), jnp.float32),
+        in_specs=[vmem],
+        out_specs=vmem,
+        scratch_shapes=[
+            pltpu.VMEM((column_count, pair_count, part, basis), jnp.bfloat16),
+            pltpu.VMEM((column_count - 1, pair_count, part, basis), jnp.bfloat16),
+            pltpu.VMEM((pair_count, part, basis), jnp.float32),
+            pltpu.VMEM((pair_count, part, basis), jnp.bfloat16),
+            pltpu.VMEM((pair_count - 1, part, basis), jnp.bfloat16),
+            pltpu.SemaphoreType.DMA((column_count,)),
+            pltpu.SemaphoreType.DMA((column_count,)),
+            pltpu.SemaphoreType.DMA((pair_count,)),
+            pltpu.SemaphoreType.DMA((pair_count,)),
+        ],
+        compiler_params=pltpu.CompilerParams(
+            collective_id=1, has_side_effects=True, vmem_limit_bytes=24 * 2**20
+        ),
+        name="reduce_rows",
+    )(gram.reshape(pair_count, column_count, part, basis))
+    return fitted, exchange
 
 
 def solution(mesh):

time: 532 us -> 252 us (0.47)
  waiting for transfers between devices: 143 us -> 0 us
  blocking collectives: 75 us -> 0 us
  Pallas kernels: 295 us -> 239 us
  between operations: 14.1 us -> 0.69 us
  local copies, waits for them, and re-layouts: 4.18 us -> 11.1 us
    reduce_scatter x1 -> x0, waiting for transfers between devices: 143 us -> none  [shards(): lax.psum_scatter(gram, ('pair', 'aux'), scatter_dimension=0, tiled=True)]
    pallas_call x1, Pallas kernels: 129 us -> 7.08 us  [shards(): pl.pallas_call(functools.partial(pack_kernel, pair_count, capacity, block...]
    all_gather x1 -> x0, blocking collectives: 75 us -> none  [shards(): whole_panel = lax.all_gather(panel, 'pair', axis=0, tiled=True)]
    pallas_call x0 -> x1, Pallas kernels: none -> 59.9 us  [shards(): pl.pallas_call(functools.partial(reduce_kernel, pair_count, column_count,...]
    unnamed x8 -> x11, local copies, waits for them, and re-layouts: 3.4 us -> 10.3 us
  transfers between devices with their start and end apart: 1 -> 0, of which waited for: 1 -> 0; matrix products, arithmetic and copies ran while one was open for 0% -> 0% of each run, Pallas kernels for 0% -> 0%
where the time goes in v2:
time: 252 us
  Pallas kernels  239 us (95%)
  local copies, waits for them, and re-layouts  11.1 us (4%)
    pallas_call x1, Pallas kernels, shards(): pl.pallas_call(functools.partial(exchange_kernel, pair_count), out_shape=...  145 us
    pallas_call x1, Pallas kernels, shards(): pl.pallas_call(functools.partial(reduce_kernel, pair_count, column_count,...  59.9 us
    pallas_call x1, Pallas kernels, shards(): pl.pallas_call(functools.partial(fit_kernel, capacity), out_shape=(jax.Sh...  27.8 us
    unnamed x11, local copies, waits for them, and re-layouts  10.3 us
    pallas_call x1, Pallas kernels, shards(): pl.pallas_call(functools.partial(pack_kernel, pair_count, capacity, block...  7.08 us

profile of v2, /device:TPU:0, one launch (start us, length us, event | category | flops | bytes accessed | tf_op | source)
XLA Modules:
  0.0 252.0 jit_solution(5292554459799112878)
XLA Ops:
  0.6 0.8 fusion
  1.4 0.7 add_bitcast_fusion.table_ref
  2.1 0.0 copy-start.2
  2.1 2.2 copy-done.2
  4.3 0.0 copy-start.4
  4.3 7.1 %pack.1 = bf16[64,32,2048]{2,1,0:T(8,128)(2,1)S(1)} custom-call(s32[8,32]{1,0:T(8,128)S(1)} %add_bitcast_fusion.table_ref, bf16[32,32,2048]{2,1,0:T(8,128)(2,1)S(1)} %copy-done.2), custom_call_target="tpu_custom_call" | custom-call | tf_op jit(solution)/shard_map/pack/pallas_call | solution.py:318
  11.4 0.0 copy-start
  11.4 3.2 %copy-done = bf16[64,32,2048]{2,1,0:T(8,128)(2,1)} copy-done((bf16[64,32,2048]{2,1,0:T(8,128)(2,1)}, bf16[64,32,2048]{2,1,0:T(8,128)(2,1)S(1)}, u32[]{:S(2)}) %copy-start) | copy-done | bytes 8388632
  14.6 144.7 %exchange_blocks.1 = (bf16[8,8,32,2048]{3,2,1,0:T(8,128)(2,1)}, bf16[512,64]{1,0:T(8,128)(2,1)}) custom-call(bf16[8,8,32,2048]{3,2,1,0:T(8,128)(2,1)} %bitcast.8, bf16[64,64]{1,0:T(8,128)(2,1)} %panel_ref.1), custom_call_target="tpu_custom_call" | custom-call | tf_op jit(solution)/shard_map/exchange_blocks/pallas_call | solution.py:331
  159.3 0.0 copy-done.4
  159.3 0.0 copy-start.1
  159.4 3.4 %copy-done.1 = bf16[8,8,32,2048]{3,2,1,0:T(8,128)(2,1)S(1)} copy-done((bf16[8,8,32,2048]{3,2,1,0:T(8,128)(2,1)S(1)}, bf16[8,8,32,2048]{3,2,1,0:T(8,128)(2,1)}, u32[]{:S(2)}) %copy-start.1) | copy-done | bytes 8388632
  162.7 0.0 copy-start.3
  162.7 0.9 copy-done.3
  163.6 27.8 %fit.1 = (bf16[1,512,4096]{2,1,0:T(8,128)(2,1)}, f32[512,512]{1,0:T(8,128)S(1)}) custom-call(s32[8,32]{1,0:T(8,128)S(1)} %add_bitcast_fusion.table_ref, bf16[512,64]{1,0:T(8,128)(2,1)S(1)} %copy-done.3, f32[1,64,64]{2,1,0:T(8,128)S(1)} %copy-done.4, bf16[64,32,2048]{2,1,0:T(8,128)(2,1)S(1)} %bitcast.9), custom_call_target="tpu_custom_call" | custom-call | tf_op jit(solution)/shard_map/fit/pallas_call | solution.py:351
  191.5 59.9 %reduce_rows.1 = f32[16,512]{1,0:T(8,128)S(1)} custom-call(f32[8,4,16,512]{3,2,1,0:T(8,128)S(1)} %bitcast.10), custom_call_target="tpu_custom_call" | custom-call | tf_op jit(solution)/shard_map/reduce_rows/pallas_call | solution.py:374
  251.4 0.6 copy.13
Async XLA Ops:
  2.1 2.2 copy-start.2
  4.3 155.0 %copy-start.4 = (f32[1,64,64]{2,1,0:T(8,128)S(1)}, f32[1,64,64]{2,1,0:T(8,128)}, u32[]{:S(2)}) copy-start(f32[1,64,64]{2,1,0:T(8,128)} %metric_ref.1) | copy-start | bytes 49156
  11.4 3.2 %copy-start = (bf16[64,32,2048]{2,1,0:T(8,128)(2,1)}, bf16[64,32,2048]{2,1,0:T(8,128)(2,1)S(1)}, u32[]{:S(2)}) copy-start(bf16[64,32,2048]{2,1,0:T(8,128)(2,1)S(1)} %pack.1) | copy-start | bytes 25165828
  159.3 3.4 %copy-start.1 = (bf16[8,8,32,2048]{3,2,1,0:T(8,128)(2,1)S(1)}, bf16[8,8,32,2048]{3,2,1,0:T(8,128)(2,1)}, u32[]{:S(2)}) copy-start(bf16[8,8,32,2048]{3,2,1,0:T(8,128)(2,1)} %get-tuple-element.7) | copy-start | bytes 25165828
  162.7 0.9 copy-start.3

commit v3 on v2

--- a/solution.py
+++ b/solution.py
@@ -12,9 +12,12 @@
 IG = 16
 
 
-def pack_kernel(pair_count, capacity, base, table_ref, tc_ref, packed_ref, counts, sems):
+def pack_kernel(
+    pair_count, capacity, base, table_ref, tc_ref, packed_ref, entries, counts, sems
+):
     me = lax.axis_index("pair")
     slot_count = tc_ref.shape[0]
+    rows = packed_ref.shape[0]
 
     def clear(i, _):
         counts[i] = 0
@@ -33,18 +36,82 @@
 
     lax.fori_loop(0, slot_count, start, 0)
 
+    def per_source(p, found):
+        def per_slot(s, carry):
+            found, rank = carry
+            code = table_ref[p, s]
+            mine = lax.div(code, base * base) == me
+
+            @pl.when(mine)
+            def _():
+                entries[0, found] = p * capacity + rank
+                entries[1, found] = lax.rem(lax.div(code, base), base)
+                entries[2, found] = lax.rem(code, base)
+
+            step = mine.astype(jnp.int32)
+            return found + step, rank + step
+
+        found, _ = lax.fori_loop(0, slot_count, per_slot, (found, 0))
+        return found
+
+    found = lax.fori_loop(0, pair_count, per_source, 0)
+    entries[0, found] = 0
+    entries[1, found] = base
+    entries[2, found] = 0
+    entries[0, rows + 1] = found
+
     def finish(s, _):
         pltpu.make_async_copy(tc_ref.at[s], packed_ref.at[0], sems.at[s]).wait()
         return 0
 
     lax.fori_loop(0, slot_count, finish, 0)
+
+
+def iota(shape, axis):
+    return lax.broadcasted_iota(jnp.int32, shape, axis)
+
+
+def build_weights(panel_ref, metric_ref, weights, metric_hi, metric_lo):
+    aux = metric_ref.shape[1]
+    orbitals = panel_ref.shape[1]
+    block_count, depth, wide = weights.shape
+    width = depth // QG
+    lanes = QG * IG
+    expand = (
+        iota((orbitals, wide), 0) == iota((orbitals, wide), 1) // QG
+    ).astype(jnp.bfloat16)
+    diagonal = iota((depth, wide), 0) // width == iota((depth, wide), 1) % QG
+    for n in range(block_count):
+        block = panel_ref[n * width : (n + 1) * width, :]
+        spread = jnp.dot(block, expand, preferred_element_type=jnp.float32)
+        spread = jnp.concatenate([spread] * QG, axis=0)
+        weights[n] = jnp.where(diagonal, spread, 0.0).astype(jnp.bfloat16)
+
+    size = aux * IG
+    metric = metric_ref[0]
+    high = metric.astype(jnp.bfloat16)
+    low = (metric - high.astype(jnp.float32)).astype(jnp.bfloat16)
+    row_aux = (iota((size, aux), 0) // lanes) * QG + iota((size, aux), 0) % QG
+    pick_row = (row_aux == iota((size, aux), 1)).astype(jnp.bfloat16)
+    pick_col = (iota((aux, size), 0) == iota((aux, size), 1) // IG).astype(jnp.bfloat16)
+    same = (iota((size, size), 0) % lanes) // QG == iota((size, size), 1) % IG
+    for part, out in ((high, metric_hi), (low, metric_lo)):
+        rows = lax.dot_general(
+            pick_row, part, (((1,), (1,)), ((), ())), preferred_element_type=jnp.float32
+        ).astype(jnp.bfloat16)
+        full = jnp.dot(rows, pick_col, preferred_element_type=jnp.float32)
+        out[...] = jnp.where(same, full, 0.0).astype(jnp.bfloat16)
 
 
 def exchange_kernel(
     n,
     packed_ref,
     panel_ref,
+    metric_ref,
     recv_ref,
+    weights,
+    metric_hi,
+    metric_lo,
     whole_ref,
     send_sems,
     recv_sems,
@@ -61,7 +128,7 @@
             barrier, inc=1, device_id={"pair": lax.rem(me + k, n)}, device_id_type=MESH
         )
     pl.semaphore_wait(barrier, n - 1)
-    copies = []
+    panels = []
     for k in range(1, n):
         copy = pltpu.make_async_remote_copy(
             src_ref=panel_ref,
@@ -72,8 +139,9 @@
             device_id_type=MESH,
         )
         copy.start()
-        copies.append(copy)
-    for k in range(1, n):
+        panels.append(copy)
+    copies = []
+    for k in sorted(range(1, n), key=lambda k: abs(2 * k - n)):
         dst = lax.rem(me + k, n)
         copy = pltpu.make_async_remote_copy(
             src_ref=packed_ref.at[dst],
@@ -88,97 +156,34 @@
     own = pltpu.make_async_copy(packed_ref.at[me], recv_ref.at[me], own_sem)
     own.start()
     whole_ref[mine, :] = panel_ref[...]
+    for copy in panels:
+        copy.wait()
+    build_weights(whole_ref, metric_ref, weights, metric_hi, metric_lo)
     own.wait()
     for copy in copies:
         copy.wait()
 
 
-def iota(shape, axis):
-    return lax.broadcasted_iota(jnp.int32, shape, axis)
-
-
 def fit_kernel(
-    capacity,
-    table_ref,
-    panel_ref,
-    metric_ref,
-    recv_ref,
-    fitted_ref,
-    gram_ref,
-    recv_buf,
+    block_count,
+    orbitals,
+    entries,
     weights,
     metric_hi,
     metric_lo,
+    recv_buf,
+    fitted_ref,
+    gram_ref,
     coeff,
-    entries,
-    recv_sem,
 ):
-    me = lax.axis_index("pair")
-    pair_count, slot_count = table_ref.shape
     width = recv_buf.shape[1]
-    aux = metric_ref.shape[1]
-    orbitals = panel_ref.shape[1]
-    basis = panel_ref.shape[0]
-    block_count = basis // width
-    chunks = aux // QG
+    basis = block_count * width
+    chunks, _, wide = coeff.shape
     groups = orbitals // IG
     depth = QG * width
-    wide = QG * orbitals
     lanes = QG * IG
-
-    load = pltpu.make_async_copy(recv_ref, recv_buf, recv_sem)
-    load.start()
-
-    def per_source(p, found):
-        def per_slot(s, carry):
-            found, rank = carry
-            code = table_ref[p, s]
-            mine = lax.div(code, block_count * block_count) == me
-
-            @pl.when(mine)
-            def _():
-                entries[0, found] = p * capacity + rank
-                entries[1, found] = lax.rem(lax.div(code, block_count), block_count)
-                entries[2, found] = lax.rem(code, block_count)
-
-            step = mine.astype(jnp.int32)
-            return found + step, rank + step
-
-        found, _ = lax.fori_loop(0, slot_count, per_slot, (found, 0))
-        return found
-
-    found = lax.fori_loop(0, pair_count, per_source, 0)
-    entries[0, found] = 0
-    entries[1, found] = block_count
-    entries[2, found] = 0
-
-    expand = (
-        iota((orbitals, wide), 0) == iota((orbitals, wide), 1) // QG
-    ).astype(jnp.bfloat16)
-    diagonal = iota((depth, wide), 0) // width == iota((depth, wide), 1) % QG
-    for n in range(block_count):
-        block = panel_ref[n * width : (n + 1) * width, :]
-        spread = jnp.dot(block, expand, preferred_element_type=jnp.float32)
-        spread = jnp.concatenate([spread] * QG, axis=0)
-        weights[n] = jnp.where(diagonal, spread, 0.0).astype(jnp.bfloat16)
-
-    size = aux * IG
-    metric = metric_ref[0]
-    high = metric.astype(jnp.bfloat16)
-    low = (metric - high.astype(jnp.float32)).astype(jnp.bfloat16)
-    row_aux = (iota((size, aux), 0) // lanes) * QG + iota((size, aux), 0) % QG
-    pick_row = (row_aux == iota((size, aux), 1)).astype(jnp.bfloat16)
-    pick_col = (iota((aux, size), 0) == iota((aux, size), 1) // IG).astype(jnp.bfloat16)
-    same = (iota((size, size), 0) % lanes) // QG == iota((size, size), 1) % IG
-    for part, out in ((high, metric_hi), (low, metric_lo)):
-        rows = lax.dot_general(
-            pick_row, part, (((1,), (1,)), ((), ())), preferred_element_type=jnp.float32
-        ).astype(jnp.bfloat16)
-        full = jnp.dot(rows, pick_col, preferred_element_type=jnp.float32)
-        out[...] = jnp.where(same, full, 0.0).astype(jnp.bfloat16)
-
+    found = entries[0, recv_buf.shape[0] + 1]
     coeff[...] = jnp.zeros_like(coeff)
-    load.wait()
 
     def add(k):
         entry, mu, nu = entries[0, k], entries[1, k], entries[2, k]
@@ -315,11 +320,17 @@
     vmem = pl.BlockSpec(memory_space=pltpu.VMEM)
     hbm = pl.BlockSpec(memory_space=pl.ANY)
 
-    packed = pl.pallas_call(
+    size = aux * IG
+    depth, wide = QG * width, QG * orbitals
+
+    packed, entries = pl.pallas_call(
         functools.partial(pack_kernel, pair_count, capacity, block_count),
-        out_shape=jax.ShapeDtypeStruct((rows, width, flat), jnp.bfloat16),
+        out_shape=(
+            jax.ShapeDtypeStruct((rows, width, flat), jnp.bfloat16),
+            jax.ShapeDtypeStruct((3, rows + 2), jnp.int32),
+        ),
         in_specs=[smem, hbm],
-        out_specs=vmem,
+        out_specs=(vmem, smem),
         scratch_shapes=[
             pltpu.SMEM((pair_count,), jnp.int32),
             pltpu.SemaphoreType.DMA((slot_count,)),
@@ -328,46 +339,44 @@
         name="pack",
     )(table, three_center)
 
-    received, whole_panel = pl.pallas_call(
+    received, weights, metric_hi, metric_lo = pl.pallas_call(
         functools.partial(exchange_kernel, pair_count),
         out_shape=(
             jax.ShapeDtypeStruct((pair_count, capacity, width, flat), jnp.bfloat16),
-            jax.ShapeDtypeStruct((basis, orbitals), jnp.bfloat16),
-        ),
-        in_specs=[hbm, vmem],
-        out_specs=(hbm, vmem),
+            jax.ShapeDtypeStruct((block_count, depth, wide), jnp.bfloat16),
+            jax.ShapeDtypeStruct((size, size), jnp.bfloat16),
+            jax.ShapeDtypeStruct((size, size), jnp.bfloat16),
+        ),
+        in_specs=[vmem, vmem, vmem],
+        out_specs=(vmem, vmem, vmem, vmem),
         scratch_shapes=[
+            pltpu.VMEM((basis, orbitals), jnp.bfloat16),
             pltpu.SemaphoreType.DMA((pair_count,)),
             pltpu.SemaphoreType.DMA((pair_count,)),
             pltpu.SemaphoreType.DMA((pair_count,)),
             pltpu.SemaphoreType.DMA((pair_count,)),
             pltpu.SemaphoreType.DMA,
         ],
-        compiler_params=pltpu.CompilerParams(collective_id=0, has_side_effects=True),
+        compiler_params=pltpu.CompilerParams(
+            collective_id=0, has_side_effects=True, vmem_limit_bytes=28 * 2**20
+        ),
         name="exchange_blocks",
-    )(packed.reshape(pair_count, capacity, width, flat), panel)
-
-    size = aux * IG
+    )(packed.reshape(pair_count, capacity, width, flat), panel, metric)
+
     fitted, gram = pl.pallas_call(
-        functools.partial(fit_kernel, capacity),
+        functools.partial(fit_kernel, block_count, orbitals),
         out_shape=(
             jax.ShapeDtypeStruct((1, basis, aux * orbitals), jnp.bfloat16),
             jax.ShapeDtypeStruct((basis, basis), jnp.float32),
         ),
-        in_specs=[smem, vmem, vmem, hbm],
+        in_specs=[smem, vmem, vmem, vmem, vmem],
         out_specs=(vmem, vmem),
         scratch_shapes=[
-            pltpu.VMEM((rows, width, flat), jnp.bfloat16),
-            pltpu.VMEM((block_count, QG * width, QG * orbitals), jnp.bfloat16),
-            pltpu.VMEM((size, size), jnp.bfloat16),
-            pltpu.VMEM((size, size), jnp.bfloat16),
-            pltpu.VMEM((aux // QG, basis + width, QG * orbitals), jnp.float32),
-            pltpu.SMEM((3, rows + 8), jnp.int32),
-            pltpu.SemaphoreType.DMA,
+            pltpu.VMEM((aux // QG, basis + width, wide), jnp.float32),
         ],
-        compiler_params=pltpu.CompilerParams(vmem_limit_bytes=44 * 2**20),
+        compiler_params=pltpu.CompilerParams(vmem_limit_bytes=36 * 2**20),
         name="fit",
-    )(table, whole_panel, metric, received.reshape(rows, width, flat))
+    )(entries, weights, metric_hi, metric_lo, received.reshape(rows, width, flat))
 
     norm_factor = 1.0 / (pair_count * column_count * aux * orbitals)
     part = basis // (pair_count * column_count)

time: 252 us -> 244 us (0.968)
  Pallas kernels: 239 us -> 235 us
  local copies, waits for them, and re-layouts: 11.1 us -> 7.79 us
    pallas_call x1, Pallas kernels: 27.8 us -> 20.7 us  [shards(): pl.pallas_call(functools.partial(fit_kernel, block_count, orbitals), out_...]
    pallas_call x1, Pallas kernels: 7.08 us -> 11.5 us  [shards(): pl.pallas_call(functools.partial(pack_kernel, pair_count, capacity, block...]
    pallas_call x1, Pallas kernels: 59.9 us -> 56.4 us  [shards(): pl.pallas_call(functools.partial(reduce_kernel, pair_count, column_count,...]
    unnamed x11, local copies, waits for them, and re-layouts: 10.3 us -> 7.01 us
where the time goes in v3:
time: 244 us
  Pallas kernels  235 us (96%)
  local copies, waits for them, and re-layouts  7.79 us (3%)
    pallas_call x1, Pallas kernels, shards(): pl.pallas_call(functools.partial(exchange_kernel, pair_count), out_shape=...  146 us
    pallas_call x1, Pallas kernels, shards(): pl.pallas_call(functools.partial(reduce_kernel, pair_count, column_count,...  56.4 us
    pallas_call x1, Pallas kernels, shards(): pl.pallas_call(functools.partial(fit_kernel, block_count, orbitals), out_...  20.7 us
    pallas_call x1, Pallas kernels, shards(): pl.pallas_call(functools.partial(pack_kernel, pair_count, capacity, block...  11.5 us
    unnamed x11, local copies, waits for them, and re-layouts  7.01 us

profile of v3, /device:TPU:0, one launch (start us, length us, event | category | flops | bytes accessed | tf_op | source)
XLA Modules:
  0.0 244.0 jit_solution(5745323847622224438)
XLA Ops:
  0.6 0.0 copy-start.3
  0.6 0.8 fusion
  1.4 0.7 add_bitcast_fusion.table_ref
  2.1 0.0 copy-start.2
  2.1 2.2 copy-done.2
  4.3 0.0 copy-start.4
  4.3 11.5 %pack.1 = (bf16[64,32,2048]{2,1,0:T(8,128)(2,1)S(1)}, s32[3,66]{1,0:T(4,128)S(1)}) custom-call(s32[8,32]{1,0:T(8,128)S(1)} %add_bitcast_fusion.table_ref, bf16[32,32,2048]{2,1,0:T(8,128)(2,1)S(1)} %copy-done.2), custom_call_target="tpu_custom_call" | custom-call | tf_op jit(solution)/shard_map/pack/pallas_call | solution.py:326
  15.8 0.0 copy-done.3
  15.9 0.0 copy-done.4
  15.9 146.1 %exchange_blocks.1 = (bf16[8,8,32,2048]{3,2,1,0:T(8,128)(2,1)S(1)}, bf16[16,256,512]{2,1,0:T(8,128)(2,1)S(1)}, bf16[1024,1024]{1,0:T(8,128)(2,1)S(1)}, bf16[1024,1024]{1,0:T(8,128)(2,1)S(1)}) custom-call(bf16[8,8,32,2048]{3,2,1,0:T(8,128)(2,1)S(1)} %bitcast.9, bf16[64,64]{1,0:T(8,128)(2,1)S(1)} %copy-done.4, f32[1,64,64]{2,1,0:T(8,128)S(1)} %copy-done.3), custom_call_target="tpu_custom_call" | custom-call | tf_op jit(solution)/shard_map/exchange_blocks/pallas_call | solution.py:342
  162.0 0.0 copy-start
  162.0 2.0 copy-done
  164.0 0.0 copy-start.1
  164.0 2.2 copy-done.1
  166.2 20.7 %fit.1 = (bf16[1,512,4096]{2,1,0:T(8,128)(2,1)}, f32[512,512]{1,0:T(8,128)S(1)}) custom-call(s32[3,66]{1,0:T(4,128)S(1)} %get-tuple-element.10.entries, bf16[16,256,512]{2,1,0:T(8,128)(2,1)S(1)} %copy-done.1, bf16[1024,1024]{1,0:T(8,128)(2,1)S(1)} %get-tuple-element.13.metric_hi, bf16[1024,1024]{1,0:T(8,128)(2,1)S(1)} %get-tuple-element.14.metric_lo, ...), custom_call_target="tpu_custom_call" | custom-call | tf_op jit(solution)/shard_map/fit/pallas_call | solution.py:366
  186.9 56.4 %reduce_rows.1 = f32[16,512]{1,0:T(8,128)S(1)} custom-call(f32[8,4,16,512]{3,2,1,0:T(8,128)S(1)} %bitcast.10), custom_call_target="tpu_custom_call" | custom-call | tf_op jit(solution)/shard_map/reduce_rows/pallas_call | solution.py:383
  243.3 0.6 copy.13
Async XLA Ops:
  0.6 15.2 %copy-start.3 = (f32[1,64,64]{2,1,0:T(8,128)S(1)}, f32[1,64,64]{2,1,0:T(8,128)}, u32[]{:S(2)}) copy-start(f32[1,64,64]{2,1,0:T(8,128)} %metric_ref.1) | copy-start | bytes 49156
  2.1 2.2 copy-start.2
  4.3 11.5 %copy-start.4 = (bf16[64,64]{1,0:T(8,128)(2,1)S(1)}, bf16[64,64]{1,0:T(8,128)(2,1)}, u32[]{:S(2)}) copy-start(bf16[64,64]{1,0:T(8,128)(2,1)} %panel_ref.1) | copy-start | bytes 24580
  162.0 2.0 copy-start
  164.0 2.2 copy-start.1

commit v4 on v3

--- a/solution.py
+++ b/solution.py
@@ -13,11 +13,12 @@
 
 
 def pack_kernel(
-    pair_count, capacity, base, table_ref, tc_ref, packed_ref, entries, counts, sems
+    pair_count, capacity, spill, base, table_ref, tc_ref, packed_ref, entries, counts, sems
 ):
     me = lax.axis_index("pair")
     slot_count = tc_ref.shape[0]
-    rows = packed_ref.shape[0]
+    direct = pair_count * capacity
+    last = entries.shape[1] - 1
 
     def clear(i, _):
         counts[i] = 0
@@ -25,31 +26,39 @@
 
     lax.fori_loop(0, pair_count, clear, 0)
 
-    def start(s, _):
+    def start(s, extra):
         target = lax.div(table_ref[me, s], base * base)
         rank = counts[target]
         counts[target] = rank + 1
-        pltpu.make_async_copy(
-            tc_ref.at[s], packed_ref.at[target * capacity + rank], sems.at[s]
-        ).start()
-        return 0
+        over = rank >= capacity
+        place = jnp.where(over, direct + extra, target * capacity + rank)
+        place = jnp.minimum(place, direct + spill - 1)
+        pltpu.make_async_copy(tc_ref.at[s], packed_ref.at[place], sems.at[s]).start()
+        return extra + over.astype(jnp.int32)
 
     lax.fori_loop(0, slot_count, start, 0)
 
     def per_source(p, found):
+        lax.fori_loop(0, pair_count, clear, 0)
+
         def per_slot(s, carry):
-            found, rank = carry
+            found, extra = carry
             code = table_ref[p, s]
-            mine = lax.div(code, base * base) == me
+            target = lax.div(code, base * base)
+            rank = counts[target]
+            counts[target] = rank + 1
+            over = rank >= capacity
+            mine = target == me
 
             @pl.when(mine)
             def _():
-                entries[0, found] = p * capacity + rank
+                entries[0, found] = jnp.where(
+                    over, direct + p * spill + extra, p * capacity + rank
+                )
                 entries[1, found] = lax.rem(lax.div(code, base), base)
                 entries[2, found] = lax.rem(code, base)
 
-            step = mine.astype(jnp.int32)
-            return found + step, rank + step
+            return found + mine.astype(jnp.int32), extra + over.astype(jnp.int32)
 
         found, _ = lax.fori_loop(0, slot_count, per_slot, (found, 0))
         return found
@@ -58,7 +67,7 @@
     entries[0, found] = 0
     entries[1, found] = base
     entries[2, found] = 0
-    entries[0, rows + 1] = found
+    entries[0, last] = found
 
     def finish(s, _):
         pltpu.make_async_copy(tc_ref.at[s], packed_ref.at[0], sems.at[s]).wait()
@@ -105,6 +114,8 @@
 
 def exchange_kernel(
     n,
+    capacity,
+    spill,
     packed_ref,
     panel_ref,
     metric_ref,
@@ -118,6 +129,11 @@
     panel_send,
     panel_recv,
     own_sem,
+    spill_sem,
+    hop_send,
+    hop_recv,
+    side_send,
+    side_recv,
 ):
     me = lax.axis_index("pair")
     rows = panel_ref.shape[0]
@@ -140,28 +156,149 @@
         )
         copy.start()
         panels.append(copy)
+    direct = n * capacity
+    own_spill = packed_ref.at[pl.ds(direct, spill)] if spill else None
+
+    def landing(source):
+        return recv_ref.at[pl.ds(direct + source * spill, spill)]
+
+    def forward(source, dst, first, send_sem, recv_sem):
+        return pltpu.make_async_remote_copy(
+            src_ref=own_spill if first else landing(source),
+            dst_ref=landing(source),
+            send_sem=send_sem,
+            recv_sem=recv_sem,
+            device_id={"pair": dst},
+            device_id_type=MESH,
+        )
+
+    length = n // 2
+    at = lax.div(me, 2)
+    other = me + 1 - 2 * lax.rem(me, 2)
+
+    def hop(way, h):
+        place = at if way else length - 1 - at
+        step = 2 if way else -2
+        sends = jnp.logical_and(place >= h, place < length - 1)
+        copy = forward(
+            jnp.clip(me - step * h, 0, n - 1),
+            jnp.clip(me + step, 0, n - 1),
+            h == 0,
+            hop_send.at[way * length + h],
+            hop_recv.at[way * length + h],
+        )
+        return copy, sends, place >= h + 1
+
+    def side(source, first):
+        place = lax.div(source, 2)
+        return forward(source, other, first, side_send.at[place], side_recv.at[place])
+
+    def start_hop(h):
+        for way in (0, 1):
+            copy, sends, _ = hop(way, h)
+            pl.when(sends)(copy.start)
+
+    def take_hop(h):
+        for way in (0, 1):
+            copy, _, arrives = hop(way, h)
+            source = jnp.clip(me - (2 if way else -2) * (h + 1), 0, n - 1)
+
+            @pl.when(arrives)
+            def _():
+                copy.wait_recv()
+                side(source, False).start()
+
+    own_copies = [
+        pltpu.make_async_copy(
+            packed_ref.at[pl.ds(me * capacity, capacity)],
+            recv_ref.at[pl.ds(me * capacity, capacity)],
+            own_sem,
+        )
+    ]
+    if spill:
+        own_copies.append(pltpu.make_async_copy(own_spill, landing(me), spill_sem))
+        start_hop(0)
+        side(me, True).start()
     copies = []
     for k in sorted(range(1, n), key=lambda k: abs(2 * k - n)):
         dst = lax.rem(me + k, n)
-        copy = pltpu.make_async_remote_copy(
-            src_ref=packed_ref.at[dst],
-            dst_ref=recv_ref.at[me],
-            send_sem=send_sems.at[k],
-            recv_sem=recv_sems.at[k],
-            device_id={"pair": dst},
-            device_id_type=MESH,
-        )
+        copies.append(
+            pltpu.make_async_remote_copy(
+                src_ref=packed_ref.at[pl.ds(dst * capacity, capacity)],
+                dst_ref=recv_ref.at[pl.ds(me * capacity, capacity)],
+                send_sem=send_sems.at[k],
+                recv_sem=recv_sems.at[k],
+                device_id={"pair": dst},
+                device_id_type=MESH,
+            )
+        )
+    head = 2 if spill else n - 1
+    for copy in copies[:head]:
         copy.start()
-        copies.append(copy)
-    own = pltpu.make_async_copy(packed_ref.at[me], recv_ref.at[me], own_sem)
-    own.start()
+    for copy in own_copies:
+        copy.start()
     whole_ref[mine, :] = panel_ref[...]
     for copy in panels:
         copy.wait()
     build_weights(whole_ref, metric_ref, weights, metric_hi, metric_lo)
-    own.wait()
+    if spill:
+        take_hop(0)
+        for h in range(1, length - 1):
+            start_hop(h)
+            for copy in copies[head : head + 2]:
+                copy.start()
+            head += 2
+            take_hop(h)
+        for copy in copies[head:]:
+            copy.start()
+        for h in range(length - 1):
+            for way in (0, 1):
+                copy, sends, _ = hop(way, h)
+                pl.when(sends)(copy.wait_send)
+        for place in range(length):
+            copy = forward(
+                2 * place, other, False, side_send.at[place], side_recv.at[place]
+            )
+            copy.wait()
+    for copy in own_copies:
+        copy.wait()
     for copy in copies:
         copy.wait()
+
+
+def flag_kernel(
+    columns, targets_count, capacity, screen_ref, out_ref, send, recv, send_sems, recv_sems
+):
+    col = lax.axis_index("aux")
+    barrier = pltpu.get_barrier_semaphore()
+    for k in range(1, columns):
+        pl.semaphore_signal(
+            barrier, inc=1, device_id={"aux": lax.rem(col + k, columns)}, device_id_type=MESH
+        )
+    targets = screen_ref[...]
+    beyond = jnp.zeros((targets.shape[0], 1), jnp.float32)
+    for t in range(targets_count):
+        named = jnp.sum(jnp.where(targets == t, 1.0, 0.0), axis=1, keepdims=True)
+        beyond += jnp.maximum(named - capacity, 0.0)
+    worst = jnp.zeros(out_ref.shape, jnp.float32) + jnp.max(beyond, axis=0, keepdims=True)
+    send[...] = worst
+    pl.semaphore_wait(barrier, columns - 1)
+    copies = []
+    for k in range(1, columns):
+        copy = pltpu.make_async_remote_copy(
+            src_ref=send,
+            dst_ref=recv.at[k - 1],
+            send_sem=send_sems.at[k],
+            recv_sem=recv_sems.at[k],
+            device_id={"aux": lax.rem(col + k, columns)},
+            device_id_type=MESH,
+        )
+        copy.start()
+        copies.append(copy)
+    for k, copy in enumerate(copies):
+        copy.wait()
+        worst = jnp.maximum(worst, recv[k])
+    out_ref[...] = worst
 
 
 def fit_kernel(
@@ -182,7 +319,7 @@
     groups = orbitals // IG
     depth = QG * width
     lanes = QG * IG
-    found = entries[0, recv_buf.shape[0] + 1]
+    found = entries[0, entries.shape[1] - 1]
     coeff[...] = jnp.zeros_like(coeff)
 
     def add(k):
@@ -323,60 +460,93 @@
     size = aux * IG
     depth, wide = QG * width, QG * orbitals
 
-    packed, entries = pl.pallas_call(
-        functools.partial(pack_kernel, pair_count, capacity, block_count),
-        out_shape=(
-            jax.ShapeDtypeStruct((rows, width, flat), jnp.bfloat16),
-            jax.ShapeDtypeStruct((3, rows + 2), jnp.int32),
-        ),
-        in_specs=[smem, hbm],
-        out_specs=(vmem, smem),
-        scratch_shapes=[
-            pltpu.SMEM((pair_count,), jnp.int32),
-            pltpu.SemaphoreType.DMA((slot_count,)),
-        ],
-        compiler_params=pltpu.CompilerParams(vmem_limit_bytes=16 * 2**20),
-        name="pack",
-    )(table, three_center)
-
-    received, weights, metric_hi, metric_lo = pl.pallas_call(
-        functools.partial(exchange_kernel, pair_count),
-        out_shape=(
-            jax.ShapeDtypeStruct((pair_count, capacity, width, flat), jnp.bfloat16),
-            jax.ShapeDtypeStruct((block_count, depth, wide), jnp.bfloat16),
-            jax.ShapeDtypeStruct((size, size), jnp.bfloat16),
-            jax.ShapeDtypeStruct((size, size), jnp.bfloat16),
-        ),
-        in_specs=[vmem, vmem, vmem],
-        out_specs=(vmem, vmem, vmem, vmem),
-        scratch_shapes=[
-            pltpu.VMEM((basis, orbitals), jnp.bfloat16),
-            pltpu.SemaphoreType.DMA((pair_count,)),
-            pltpu.SemaphoreType.DMA((pair_count,)),
-            pltpu.SemaphoreType.DMA((pair_count,)),
-            pltpu.SemaphoreType.DMA((pair_count,)),
-            pltpu.SemaphoreType.DMA,
-        ],
-        compiler_params=pltpu.CompilerParams(
-            collective_id=0, has_side_effects=True, vmem_limit_bytes=28 * 2**20
-        ),
-        name="exchange_blocks",
-    )(packed.reshape(pair_count, capacity, width, flat), panel, metric)
-
-    fitted, gram = pl.pallas_call(
-        functools.partial(fit_kernel, block_count, orbitals),
-        out_shape=(
-            jax.ShapeDtypeStruct((1, basis, aux * orbitals), jnp.bfloat16),
-            jax.ShapeDtypeStruct((basis, basis), jnp.float32),
-        ),
-        in_specs=[smem, vmem, vmem, vmem, vmem],
-        out_specs=(vmem, vmem),
-        scratch_shapes=[
-            pltpu.VMEM((aux // QG, basis + width, wide), jnp.float32),
-        ],
-        compiler_params=pltpu.CompilerParams(vmem_limit_bytes=36 * 2**20),
-        name="fit",
-    )(entries, weights, metric_hi, metric_lo, received.reshape(rows, width, flat))
+    def fit(part, spill, table, three_center, panel, metric):
+        packed, entries = pl.pallas_call(
+            functools.partial(pack_kernel, pair_count, part, spill, block_count),
+            out_shape=(
+                jax.ShapeDtypeStruct((pair_count * part + spill, width, flat), jnp.bfloat16),
+                jax.ShapeDtypeStruct((3, rows + 2), jnp.int32),
+            ),
+            in_specs=[smem, hbm],
+            out_specs=(vmem, smem),
+            scratch_shapes=[
+                pltpu.SMEM((pair_count,), jnp.int32),
+                pltpu.SemaphoreType.DMA((slot_count,)),
+            ],
+            compiler_params=pltpu.CompilerParams(vmem_limit_bytes=16 * 2**20),
+            name="pack",
+        )(table, three_center)
+
+        received, weights, metric_hi, metric_lo = pl.pallas_call(
+            functools.partial(exchange_kernel, pair_count, part, spill),
+            out_shape=(
+                jax.ShapeDtypeStruct((pair_count * (part + spill), width, flat), jnp.bfloat16),
+                jax.ShapeDtypeStruct((block_count, depth, wide), jnp.bfloat16),
+                jax.ShapeDtypeStruct((size, size), jnp.bfloat16),
+                jax.ShapeDtypeStruct((size, size), jnp.bfloat16),
+            ),
+            in_specs=[vmem, vmem, vmem],
+            out_specs=(vmem, vmem, vmem, vmem),
+            scratch_shapes=[
+                pltpu.VMEM((basis, orbitals), jnp.bfloat16),
+                pltpu.SemaphoreType.DMA((pair_count,)),
+                pltpu.SemaphoreType.DMA((pair_count,)),
+                pltpu.SemaphoreType.DMA((pair_count,)),
+                pltpu.SemaphoreType.DMA((pair_count,)),
+                pltpu.SemaphoreType.DMA,
+                pltpu.SemaphoreType.DMA,
+                pltpu.SemaphoreType.DMA((pair_count,)),
+                pltpu.SemaphoreType.DMA((pair_count,)),
+                pltpu.SemaphoreType.DMA((pair_count,)),
+                pltpu.SemaphoreType.DMA((pair_count,)),
+            ],
+            compiler_params=pltpu.CompilerParams(
+                collective_id=2 if spill else 0, has_side_effects=True, vmem_limit_bytes=28 * 2**20
+            ),
+            name="exchange_blocks",
+        )(packed, panel, metric)
+
+        fitted, gram = pl.pallas_call(
+            functools.partial(fit_kernel, block_count, orbitals),
+            out_shape=(
+                jax.ShapeDtypeStruct((1, basis, aux * orbitals), jnp.bfloat16),
+                jax.ShapeDtypeStruct((basis, basis), jnp.float32),
+            ),
+            in_specs=[smem, vmem, vmem, vmem, vmem],
+            out_specs=(vmem, vmem),
+            scratch_shapes=[
+                pltpu.VMEM((aux // QG, basis + width, wide), jnp.float32),
+            ],
+            compiler_params=pltpu.CompilerParams(vmem_limit_bytes=33 * 2**20),
+            name="fit",
+        )(entries, weights, metric_hi, metric_lo, received)
+        return fitted, gram
+
+    arrays = (table, three_center, panel, metric)
+    direct, spill = 5 * capacity // 8, 3 * slot_count // 16
+    if capacity < 8 or pair_count % 2:
+        fitted, gram = fit(capacity, 0, *arrays)
+    else:
+        worst = pl.pallas_call(
+            functools.partial(flag_kernel, column_count, pair_count, direct),
+            out_shape=jax.ShapeDtypeStruct((8, 128), jnp.float32),
+            in_specs=[vmem],
+            out_specs=vmem,
+            scratch_shapes=[
+                pltpu.VMEM((8, 128), jnp.float32),
+                pltpu.VMEM((column_count - 1, 8, 128), jnp.float32),
+                pltpu.SemaphoreType.DMA((column_count,)),
+                pltpu.SemaphoreType.DMA((column_count,)),
+            ],
+            compiler_params=pltpu.CompilerParams(collective_id=3, has_side_effects=True),
+            name="most_beyond",
+        )(screen[:, :, 0])
+        fitted, gram = lax.cond(
+            worst[0, 0] <= spill,
+            functools.partial(fit, direct, spill),
+            functools.partial(fit, capacity, 0),
+            *arrays,
+        )
 
     norm_factor = 1.0 / (pair_count * column_count * aux * orbitals)
     part = basis // (pair_count * column_count)

time: 244 us -> 240 us (0.984)
  local copies, waits for them, and re-layouts: 7.79 us -> 2.59 us
    pallas_call x3 -> x4, Pallas kernels: 178 us -> 221 us  [the longest x1 191 us: fit(): pl.pallas_call(functools.partial(exchange_kernel, pair_count, part, spill...]
    pallas_call x1, Pallas kernels: 56.4 us -> 14.1 us  [shards(): pl.pallas_call(functools.partial(reduce_kernel, pair_count, column_count,...]
    unnamed x11 -> x1, local copies, waits for them, and re-layouts: 7.01 us -> 0.62 us
where the time goes in v4:
time: 240 us
  Pallas kernels  235 us (98%)
  local copies, waits for them, and re-layouts  2.59 us (1%)
    pallas_call x1, Pallas kernels, fit(): pl.pallas_call(functools.partial(exchange_kernel, pair_count, part, spill...  191 us
    pallas_call x1, Pallas kernels, fit(): pl.pallas_call(functools.partial(fit_kernel, block_count, orbitals), out_...  17.4 us
    pallas_call x1, Pallas kernels, shards(): pl.pallas_call(functools.partial(reduce_kernel, pair_count, column_count,...  14.1 us
    pallas_call x1, Pallas kernels, fit(): pl.pallas_call(functools.partial(pack_kernel, pair_count, part, spill, bl...  7.05 us
    pallas_call x1, Pallas kernels, shards(): pl.pallas_call(functools.partial(flag_kernel, column_count, pair_count, d...  5.97 us

profile of v4, /device:TPU:0, one launch (start us, length us, event | category | flops | bytes accessed | tf_op | source)
XLA Modules:
  0.0 240.3 jit_solution(7370341770191859858)
XLA Ops:
  0.6 6.0 %most_beyond.1 = f32[8,128]{1,0:T(8,128)} custom-call(s32[8,32]{1,0:T(8,128)} %bitcast.10), custom_call_target="tpu_custom_call" | custom-call | tf_op jit(solution)/shard_map/most_beyond/pallas_call | solution.py:530
  6.6 1.2 slice.9
  8.4 0.8 fusion
  9.2 0.7 multiply_add_fusion
  9.9 215.6 %conditional.1 = ((bf16[1,512,4096]{2,1,0:T(8,128)(2,1)}, f32[512,512]{1,0:T(8,128)S(1)})) conditional(s32[]{:T(128)} %bitcast.1, (s32[8,32]{1,0:T(8,128)S(1)}, bf16[32,32,2048]{2,1,0:T(8,128)(2,1)}, bf16[64,64]{1,0:T(8,128)(2,1)}, f32[1,64,64]{2,1,0:T(8,128)}) %tuple.14, (s32[8,32]{1,0:T(8,128)S(1)}, bf16[32,32,2048]{2,1,0:T(8,128)(2,1)}, ...), branch_computations={%region_0.0_spmd, %region_1.0_spmd} | conditional | bytes 98368 | solution.py:544
  9.9 0.0 copy-start.1
  9.9 0.0 copy-start.3
  9.9 7.0 %pack.3 = (bf16[46,32,2048]{2,1,0:T(8,128)(2,1)S(1)}, s32[3,66]{1,0:T(4,128)S(1)}) custom-call(s32[8,32]{1,0:T(8,128)S(1)} %get-tuple-element.26.table_ref, bf16[32,32,2048]{2,1,0:T(8,128)(2,1)} %get-tuple-element.27.tc_ref), custom_call_target="tpu_custom_call" | custom-call | tf_op jit(solution)/shard_map/cond/branch_1_fun/pack/pallas_call | solution.py:464
  17.0 0.0 copy-done.1
  17.0 0.0 copy-done.3
  17.0 190.8 %exchange_blocks.3 = (bf16[88,32,2048]{2,1,0:T(8,128)(2,1)S(1)}, bf16[16,256,512]{2,1,0:T(8,128)(2,1)S(1)}, bf16[1024,1024]{1,0:T(8,128)(2,1)S(1)}, bf16[1024,1024]{1,0:T(8,128)(2,1)S(1)}) custom-call(bf16[46,32,2048]{2,1,0:T(8,128)(2,1)S(1)} %get-tuple-element.29.packed_ref, bf16[64,64]{1,0:T(8,128)(2,1)S(1)} %copy-done.3, f32[1,64,64]{2,1,0:T(8,128)S(1)} %copy-done.1), custom_call_target="tpu_custom_call" | custom-call | tf_op jit(solution)/shard_map/cond/branch_1_fun/exchange_blocks/pallas_call | solution.py:480
  207.8 17.4 %fit.3 = (bf16[1,512,4096]{2,1,0:T(8,128)(2,1)}, f32[512,512]{1,0:T(8,128)S(1)}) custom-call(s32[3,66]{1,0:T(4,128)S(1)} %get-tuple-element.28.entries, bf16[16,256,512]{2,1,0:T(8,128)(2,1)S(1)} %get-tuple-element.32.weights, bf16[1024,1024]{1,0:T(8,128)(2,1)S(1)} %get-tuple-element.33.metric_hi, bf16[1024,1024]{1,0:T(8,128)(2,1)S(1)} %get-tuple-element.34.metric_lo, ...), custom_call_target="tpu_custom_call" | custom-call | tf_op jit(solution)/shard_map/cond/branch_1_fun/fit/pallas_call | solution.py:509
  225.6 14.1 %reduce_rows.1 = f32[16,512]{1,0:T(8,128)S(1)} custom-call(f32[8,4,16,512]{3,2,1,0:T(8,128)S(1)} %bitcast.9), custom_call_target="tpu_custom_call" | custom-call | tf_op jit(solution)/shard_map/reduce_rows/pallas_call | solution.py:553
  239.7 0.6 copy.16
Async XLA Ops:
  9.9 7.1 %copy-start.1 = (f32[1,64,64]{2,1,0:T(8,128)S(1)}, f32[1,64,64]{2,1,0:T(8,128)}, u32[]{:S(2)}) copy-start(f32[1,64,64]{2,1,0:T(8,128)} %get-tuple-element.31.metric_ref) | copy-start | bytes 49156 | tf_op jit(solution)/shard_map/cond
  9.9 7.1 %copy-start.3 = (bf16[64,64]{1,0:T(8,128)(2,1)S(1)}, bf16[64,64]{1,0:T(8,128)(2,1)}, u32[]{:S(2)}) copy-start(bf16[64,64]{1,0:T(8,128)(2,1)} %get-tuple-element.30.panel_ref) | copy-start | bytes 24580 | tf_op jit(solution)/shard_map/cond

commit v5 on v4

--- a/solution.py
+++ b/solution.py
@@ -232,9 +232,9 @@
                 device_id_type=MESH,
             )
         )
-    head = 2 if spill else n - 1
-    for copy in copies[:head]:
-        copy.start()
+    if not spill:
+        for copy in copies:
+            copy.start()
     for copy in own_copies:
         copy.start()
     whole_ref[mine, :] = panel_ref[...]
@@ -242,15 +242,13 @@
         copy.wait()
     build_weights(whole_ref, metric_ref, weights, metric_hi, metric_lo)
     if spill:
-        take_hop(0)
         for h in range(1, length - 1):
+            take_hop(h - 1)
             start_hop(h)
-            for copy in copies[head : head + 2]:
-                copy.start()
-            head += 2
-            take_hop(h)
-        for copy in copies[head:]:
+        for copy in copies:
             copy.start()
+        if length > 1:
+            take_hop(length - 2)
         for h in range(length - 1):
             for way in (0, 1):
                 copy, sends, _ = hop(way, h)

time: 240 us -> 209 us (0.87)
  Pallas kernels: 235 us -> 205 us
    pallas_call x1, Pallas kernels: 191 us -> 135 us  [fit(): pl.pallas_call(functools.partial(exchange_kernel, pair_count, part, spill...]
    pallas_call x1, Pallas kernels: 14.1 us -> 39.5 us  [shards(): pl.pallas_call(functools.partial(reduce_kernel, pair_count, column_count,...]
where the time goes in v5:
time: 209 us; the launch traced here: 210 us
  Pallas kernels  205 us (98%)
  local copies, waits for them, and re-layouts  2.59 us (1%)
    pallas_call x1, Pallas kernels, fit(): pl.pallas_call(functools.partial(exchange_kernel, pair_count, part, spill...  135 us
    pallas_call x1, Pallas kernels, shards(): pl.pallas_call(functools.partial(reduce_kernel, pair_count, column_count,...  39.5 us
    pallas_call x1, Pallas kernels, fit(): pl.pallas_call(functools.partial(fit_kernel, block_count, orbitals), out_...  17.4 us
    pallas_call x1, Pallas kernels, fit(): pl.pallas_call(functools.partial(pack_kernel, pair_count, part, spill, bl...  7.05 us
    pallas_call x1, Pallas kernels, shards(): pl.pallas_call(functools.partial(flag_kernel, column_count, pair_count, d...  5.97 us

profile of v5, /device:TPU:0, one launch (start us, length us, event | category | flops | bytes accessed | tf_op | source)
XLA Modules:
  0.0 209.9 jit_solution(10247988488874063876)
XLA Ops:
  0.6 6.0 %most_beyond.1 = f32[8,128]{1,0:T(8,128)} custom-call(s32[8,32]{1,0:T(8,128)} %bitcast.10), custom_call_target="tpu_custom_call" | custom-call | tf_op jit(solution)/shard_map/most_beyond/pallas_call | solution.py:528
  6.6 1.2 slice.9
  8.4 0.8 fusion
  9.2 0.7 multiply_add_fusion
  9.9 159.8 %conditional.1 = ((bf16[1,512,4096]{2,1,0:T(8,128)(2,1)}, f32[512,512]{1,0:T(8,128)S(1)})) conditional(s32[]{:T(128)} %bitcast.1, (s32[8,32]{1,0:T(8,128)S(1)}, bf16[32,32,2048]{2,1,0:T(8,128)(2,1)}, bf16[64,64]{1,0:T(8,128)(2,1)}, f32[1,64,64]{2,1,0:T(8,128)}) %tuple.14, (s32[8,32]{1,0:T(8,128)S(1)}, bf16[32,32,2048]{2,1,0:T(8,128)(2,1)}, ...), branch_computations={%region_0.0_spmd, %region_1.0_spmd} | conditional | bytes 98368 | solution.py:542
  9.9 0.0 copy-start.1
  9.9 0.0 copy-start.3
  9.9 7.0 %pack.3 = (bf16[46,32,2048]{2,1,0:T(8,128)(2,1)S(1)}, s32[3,66]{1,0:T(4,128)S(1)}) custom-call(s32[8,32]{1,0:T(8,128)S(1)} %get-tuple-element.26.table_ref, bf16[32,32,2048]{2,1,0:T(8,128)(2,1)} %get-tuple-element.27.tc_ref), custom_call_target="tpu_custom_call" | custom-call | tf_op jit(solution)/shard_map/cond/branch_1_fun/pack/pallas_call | solution.py:462
  17.0 0.0 copy-done.1
  17.0 0.0 copy-done.3
  17.0 135.0 %exchange_blocks.3 = (bf16[88,32,2048]{2,1,0:T(8,128)(2,1)S(1)}, bf16[16,256,512]{2,1,0:T(8,128)(2,1)S(1)}, bf16[1024,1024]{1,0:T(8,128)(2,1)S(1)}, bf16[1024,1024]{1,0:T(8,128)(2,1)S(1)}) custom-call(bf16[46,32,2048]{2,1,0:T(8,128)(2,1)S(1)} %get-tuple-element.29.packed_ref, bf16[64,64]{1,0:T(8,128)(2,1)S(1)} %copy-done.3, f32[1,64,64]{2,1,0:T(8,128)S(1)} %copy-done.1), custom_call_target="tpu_custom_call" | custom-call | tf_op jit(solution)/shard_map/cond/branch_1_fun/exchange_blocks/pallas_call | solution.py:478
  152.0 17.4 %fit.3 = (bf16[1,512,4096]{2,1,0:T(8,128)(2,1)}, f32[512,512]{1,0:T(8,128)S(1)}) custom-call(s32[3,66]{1,0:T(4,128)S(1)} %get-tuple-element.28.entries, bf16[16,256,512]{2,1,0:T(8,128)(2,1)S(1)} %get-tuple-element.32.weights, bf16[1024,1024]{1,0:T(8,128)(2,1)S(1)} %get-tuple-element.33.metric_hi, bf16[1024,1024]{1,0:T(8,128)(2,1)S(1)} %get-tuple-element.34.metric_lo, ...), custom_call_target="tpu_custom_call" | custom-call | tf_op jit(solution)/shard_map/cond/branch_1_fun/fit/pallas_call | solution.py:507
  169.8 39.5 %reduce_rows.1 = f32[16,512]{1,0:T(8,128)S(1)} custom-call(f32[8,4,16,512]{3,2,1,0:T(8,128)S(1)} %bitcast.9), custom_call_target="tpu_custom_call" | custom-call | tf_op jit(solution)/shard_map/reduce_rows/pallas_call | solution.py:551
  209.3 0.6 copy.16
Async XLA Ops:
  9.9 7.1 %copy-start.1 = (f32[1,64,64]{2,1,0:T(8,128)S(1)}, f32[1,64,64]{2,1,0:T(8,128)}, u32[]{:S(2)}) copy-start(f32[1,64,64]{2,1,0:T(8,128)} %get-tuple-element.31.metric_ref) | copy-start | bytes 49156 | tf_op jit(solution)/shard_map/cond
  9.9 7.1 %copy-start.3 = (bf16[64,64]{1,0:T(8,128)(2,1)S(1)}, bf16[64,64]{1,0:T(8,128)(2,1)}, u32[]{:S(2)}) copy-start(bf16[64,64]{1,0:T(8,128)(2,1)} %get-tuple-element.30.panel_ref) | copy-start | bytes 24580 | tf_op jit(solution)/shard_map/cond
